TPU v7x, 32 devices: a whole 2x2x4 slice. The times are simulated.
32 devices in a mesh: groups: 2 (over x), rows: 16 (over z, y, core).
Axes of the slice: x: 2, y: 2, z: 4, core: 2. Of those that a mesh axis runs over, the one named last changes fastest.
Arguments:
- pair: bfloat16 [512, 256, 128], P(('groups', 'rows')), parts along dimension 0, may hold values from -6 to 6
- proj_weights: bfloat16 [6, 128, 128], replicated, may hold values from -0.5 to 0.5
- cotangent: bfloat16 [512, 256, 128], P(('groups', 'rows')), parts along dimension 0, may hold values from -8.5 to 8.5
Outputs:
- update: bfloat16 [512, 256, 128], P(('groups', 'rows')), parts along dimension 0
- pair_grad: bfloat16 [512, 256, 128], P(('groups', 'rows')), parts along dimension 0
- weight_grads: float32 [12, 128, 128], P('groups'), parts along dimension 0
There are 2 independent parts, one for each index of `groups`. A program takes and returns all parts, laid end to end along the dimension named above; an argument that names none is the same for every part. Nothing has to cross between parts.
All inputs are finite; a program needn't handle non-finite values.
Results may differ from a plain program's by a relative error of at most 0.015.
Values may be sent and summed in bfloat16 or wider, within the bound.
A program may use at most 128 MiB of HBM per device.

v0:
```python
import jax
import jax.numpy as jnp
from jax import lax
from jax.sharding import PartitionSpec as P


def layer_norm(values, along_dim):
    centred = values - jnp.mean(values, axis=along_dim, keepdims=True)
    inv_scale = lax.rsqrt(jnp.mean(centred * centred, axis=along_dim, keepdims=True) + 1e-05)
    return (centred * inv_scale, inv_scale)


def norm_backward(normed, inv_scale, upstream, along_dim):
    return (
        upstream
        - jnp.mean(upstream, axis=along_dim, keepdims=True)
        - normed * jnp.mean(upstream * normed, axis=along_dim, keepdims=True)
    ) * inv_scale


def triangle_slab(pieces):
    left_slab, right_slab = pieces
    product = lax.dot_general(
        left_slab, right_slab, (((3,), (3,)), ((0, 1), (0, 1))), preferred_element_type=jnp.float32
    )
    return (product.astype(jnp.bfloat16), left_slab, right_slab)


def edge_backward(upstream, left_slab, right_slab):
    left_part = lax.dot_general(
        upstream, right_slab, (((3,), (2,)), ((0, 1), (0, 1))), preferred_element_type=jnp.float32
    )
    right_part = lax.dot_general(
        upstream, left_slab, (((2,), (2,)), ((0, 1), (0, 1))), preferred_element_type=jnp.float32
    )
    return (left_part.astype(jnp.bfloat16), right_part.astype(jnp.bfloat16))


def body(pair, proj_weights, cotangent):
    residues = pair.shape[1]
    local_rows = pair.shape[0]
    chans = pair.shape[2]
    ranks = lax.axis_size("rows")
    slab_width = chans // ranks
    normed_in, scale_in = layer_norm(pair.astype(jnp.float32), 2)
    normed_bf = normed_in.astype(jnp.bfloat16)
    edge_pre = jnp.einsum(
        "ikd,ndc->ncik", normed_bf, proj_weights[0:4], preferred_element_type=jnp.float32
    )
    gate_pre = jnp.einsum(
        "ikd,dc->ikc", normed_bf, proj_weights[4], preferred_element_type=jnp.float32
    )
    left_sig = jax.nn.sigmoid(edge_pre[1])
    right_sig = jax.nn.sigmoid(edge_pre[3])
    left_edge = (
        (left_sig * edge_pre[0])
        .astype(jnp.bfloat16)
        .reshape(ranks, slab_width, local_rows, residues)
    )
    right_edge = (
        (right_sig * edge_pre[2])
        .astype(jnp.bfloat16)
        .reshape(ranks, slab_width, local_rows, residues)
    )
    products, left_held, right_held = triangle_slab(
        (
            lax.all_to_all(left_edge, "rows", split_axis=0, concat_axis=2, tiled=True),
            lax.all_to_all(right_edge, "rows", split_axis=0, concat_axis=2, tiled=True),
        )
    )
    regrouped = lax.all_to_all(products, "rows", split_axis=2, concat_axis=0, tiled=True).reshape(
        chans, local_rows, residues
    )
    normed_mid, scale_mid = layer_norm(regrouped.astype(jnp.float32), 0)
    mid_bf = normed_mid.astype(jnp.bfloat16)
    projected = jnp.einsum(
        "cij,cd->ijd", mid_bf, proj_weights[5], preferred_element_type=jnp.float32
    )
    gating = jax.nn.sigmoid(gate_pre)
    update = (gating * projected).astype(jnp.bfloat16)
    upstream = cotangent.astype(jnp.float32)
    gated_up = (upstream * gating).astype(jnp.bfloat16)
    gate_grad = (upstream * projected * gating * (1.0 - gating)).astype(jnp.bfloat16)
    out_weights = jnp.stack(
        [
            jnp.einsum("ikd,ikc->dc", normed_bf, gate_grad, preferred_element_type=jnp.float32),
            jnp.einsum("cij,ijd->cd", mid_bf, gated_up, preferred_element_type=jnp.float32),
        ]
    )
    mid_grad = jnp.einsum(
        "ijd,cd->cij", gated_up, proj_weights[5], preferred_element_type=jnp.float32
    )
    prod_grad = norm_backward(normed_mid, scale_mid, mid_grad, 0).astype(jnp.bfloat16)
    prod_grad = prod_grad.reshape(ranks, slab_width, local_rows, residues)
    slab_grad = lax.all_to_all(prod_grad, "rows", split_axis=0, concat_axis=2, tiled=True)
    left_part, right_part = edge_backward(slab_grad, left_held, right_held)
    left_back, right_back = (
        lax.all_to_all(left_part, "rows", split_axis=2, concat_axis=0, tiled=True),
        lax.all_to_all(right_part, "rows", split_axis=2, concat_axis=0, tiled=True),
    )
    left_full = left_back.reshape(chans, local_rows, residues).astype(jnp.float32)
    right_full = right_back.reshape(chans, local_rows, residues).astype(jnp.float32)
    edge_grad = jnp.stack(
        [
            left_full * left_sig,
            left_full * edge_pre[0] * left_sig * (1.0 - left_sig),
            right_full * right_sig,
            right_full * edge_pre[2] * right_sig * (1.0 - right_sig),
        ]
    ).astype(jnp.bfloat16)
    in_weights = jnp.einsum(
        "ikd,ncik->ndc", normed_bf, edge_grad, preferred_element_type=jnp.float32
    )
    input_grad = jnp.einsum(
        "ncik,ndc->ikd", edge_grad, proj_weights[0:4], preferred_element_type=jnp.float32
    )
    input_grad = input_grad + jnp.einsum(
        "ikc,dc->ikd", gate_grad, proj_weights[4], preferred_element_type=jnp.float32
    )
    pair_grad = norm_backward(normed_in, scale_in, input_grad, 2).astype(jnp.bfloat16)
    totals = lax.psum(
        jnp.concatenate([in_weights, out_weights], axis=0).astype(jnp.bfloat16), "rows"
    ).astype(jnp.float32)
    weight_grads = totals / residues
    return (update, pair_grad, weight_grads)


def solution(mesh):
    in_specs = (P(("groups", "rows"), None, None), P(), P(("groups", "rows"), None, None))
    out_specs = (
        P(("groups", "rows"), None, None),
        P(("groups", "rows"), None, None),
        P("groups", None, None),
    )
    return jax.shard_map(body, mesh=mesh, in_specs=in_specs, out_specs=out_specs, check_vma=False)
```

profile of v0, /device:TPU:0, one launch (start us, length us, event | category | flops | bytes accessed | tf_op | source)
XLA Modules:
  0.0 318.2 jit_solution(738744233146156121)
XLA Ops:
  7.2 1.5 copy.69
  9.2 1.3 convolution_bitcast_fusion
  10.5 1.2 fusion.46
  11.7 2.0 copy-done
  13.7 1.1 copy.75
  14.8 7.4 %all-to-all-start.1 = ((bf16[16,8,16,256]{3,1,2,0:T(8,128)(2,1)}), bf16[16,8,16,256]{3,1,2,0:T(8,128)(2,1)S(1)}, u32[]{:S(2)}, u32[]{:S(2)}) async-start(bf16[16,8,16,256]{3,1,2,0:T(8,128)(2,1)} %copy.75), calls=%async_computation.1 | async-start | bytes 2097152 | tf_op jit(solution)/shard_map/all_to_all | solution.py:68
  22.2 1.1 copy.73
  23.3 21.9 %all-to-all-done.1 = bf16[16,8,16,256]{3,1,2,0:T(8,128)(2,1)S(1)} async-done(((bf16[16,8,16,256]{3,1,2,0:T(8,128)(2,1)}), bf16[16,8,16,256]{3,1,2,0:T(8,128)(2,1)S(1)}, u32[]{:S(2)}, u32[]{:S(2)}) %all-to-all-start.1) | async-done | bytes 1048608 | tf_op jit(solution)/shard_map/all_to_all | solution.py:68
  45.2 6.9 %all-to-all-start = ((bf16[16,8,16,256]{3,1,2,0:T(8,128)(2,1)}), bf16[16,8,16,256]{3,1,2,0:T(8,128)(2,1)}, u32[]{:S(2)}, u32[]{:S(2)}) async-start(bf16[16,8,16,256]{3,1,2,0:T(8,128)(2,1)} %copy.73), calls=%async_computation | async-start | bytes 2097152 | tf_op jit(solution)/shard_map/all_to_all | solution.py:67
  52.3 22.8 %all-to-all-done = bf16[16,8,16,256]{3,1,2,0:T(8,128)(2,1)} async-done(((bf16[16,8,16,256]{3,1,2,0:T(8,128)(2,1)}), bf16[16,8,16,256]{3,1,2,0:T(8,128)(2,1)}, u32[]{:S(2)}, u32[]{:S(2)}) %all-to-all-start) | async-done | bytes 1048608 | tf_op jit(solution)/shard_map/all_to_all | solution.py:67
  75.1 1.4 copy.74
  77.6 31.5 %all_to_all.72 = bf16[1,8,256,256]{3,1,0,2:T(8,128)(2,1)S(1)} all-to-all(bf16[1,8,256,256]{3,1,0,2:T(8,128)(2,1)S(1)} %copy.77), channel_id=1, replica_groups=mesh['groups'=2,'rows'=16] {'rows'}, dimensions={2} | all-to-all | bytes 2097152 | tf_op jit(solution)/shard_map/all_to_all | solution.py:71
  111.6 2.5 fusion.13
  114.1 1.6 bitcast_reduce_fusion
  115.8 1.6 fusion.47
  117.5 29.8 %all_to_all.73 = bf16[16,8,16,256]{3,1,2,0:T(8,128)(2,1)S(1)} all-to-all(bf16[16,8,16,256]{3,1,2,0:T(8,128)(2,1)S(1)} %copy.82), channel_id=1, replica_groups=mesh['groups'=2,'rows'=16] {'rows'}, dimensions={0} | all-to-all | bytes 2097152 | tf_op jit(solution)/shard_map/all_to_all | solution.py:95
  147.3 1.0 copy-done.4
  149.0 1.6 copy.84
  150.6 5.0 %all-to-all-start.4 = ((bf16[1,8,256,256]{3,1,0,2:T(8,128)(2,1)}), bf16[1,8,256,256]{3,1,0,2:T(8,128)(2,1)}, u32[]{:S(2)}, u32[]{:S(2)}) async-start(bf16[1,8,256,256]{3,1,0,2:T(8,128)(2,1)} %copy.84), calls=%async_computation.4 | async-start | bytes 2097152 | tf_op jit(solution)/shard_map/all_to_all | solution.py:98
  155.6 2.0 fusion.36
  157.7 1.6 copy.87
  159.3 19.3 %all-to-all-done.4 = bf16[1,8,256,256]{3,1,0,2:T(8,128)(2,1)} async-done(((bf16[1,8,256,256]{3,1,0,2:T(8,128)(2,1)}), bf16[1,8,256,256]{3,1,0,2:T(8,128)(2,1)}, u32[]{:S(2)}, u32[]{:S(2)}) %all-to-all-start.4) | async-done | bytes 1048608 | tf_op jit(solution)/shard_map/all_to_all | solution.py:98
  178.6 6.9 %all-to-all-start.5 = ((bf16[1,8,256,256]{3,1,0,2:T(8,128)(2,1)}), bf16[1,8,256,256]{3,1,0,2:T(8,128)(2,1)}, u32[]{:S(2)}, u32[]{:S(2)}) async-start(bf16[1,8,256,256]{3,1,0,2:T(8,128)(2,1)} %copy.87), calls=%async_computation.5 | async-start | bytes 2097152 | tf_op jit(solution)/shard_map/all_to_all | solution.py:99
  185.8 2.0 fusion.43
  187.8 2.9 fusion.42
  190.7 17.8 %all-to-all-done.5 = bf16[1,8,256,256]{3,1,0,2:T(8,128)(2,1)} async-done(((bf16[1,8,256,256]{3,1,0,2:T(8,128)(2,1)}), bf16[1,8,256,256]{3,1,0,2:T(8,128)(2,1)}, u32[]{:S(2)}, u32[]{:S(2)}) %all-to-all-start.5) | async-done | bytes 1048608 | tf_op jit(solution)/shard_map/all_to_all | solution.py:99
  208.5 5.0 %fusion.24 = (bf16[1,128,16,256]{3,1,0,2:T(8,128)(2,1)S(1)}, bf16[1,128,16,256]{3,1,0,2:T(8,128)(2,1)S(1)}, bf16[1,128,16,256]{3,1,0,2:T(8,128)(2,1)S(1)}, bf16[1,128,16,256]{3,1,0,2:T(8,128)(2,1)S(1)}) fusion(f32[4,128,16,256]{3,1,0,2:T(8,128)} %copy-done, bf16[1,8,16,16,256]{4,1,3,2,0:T(8,128)(2,1)} %bitcast.53, bf16[1,8,16,16,256]{4,1,3,2,0:T(8,128)(2,1)} %bitcast.51), kind=kLoop, calls=%fused_computation.37 | loop fusion | flops 11534336 | bytes 14680064 | tf_op jit(solution)/shard_map/convert.17
  213.5 1.3 fusion.39
  217.5 1.6 fusion.8
  219.1 2.3 copy.93
  221.3 88.2 %all-reduce.2.cloned.1.call-done = bf16[6,128,128]{1,2,0:T(8,128)(2,1)} async-done(((bf16[6,128,128]{1,2,0:T(8,128)(2,1)}), bf16[6,128,128]{1,2,0:T(8,128)(2,1)}) %all-reduce.2.cloned.1.call-update) | async-done | bytes 196624 | tf_op jit(solution)/shard_map/psum | solution.py:121
  309.5 1.0 convert_multiply_fusion.2
  (45 shorter events, 8.8 us)
Async XLA Ops:
  7.2 2.1 copy-start.9
  10.5 3.2 %copy-start = (f32[4,128,16,256]{3,1,0,2:T(8,128)}, f32[4,128,16,256]{3,1,0,2:T(8,128)S(1)}, u32[]{:S(2)}) copy-start(f32[4,128,16,256]{3,1,0,2:T(8,128)S(1)} %convolution_bitcast_fusion) | copy-start | bytes 25165828
  14.8 30.3 %all-to-all-start.1 = ((bf16[16,8,16,256]{3,1,2,0:T(8,128)(2,1)}), bf16[16,8,16,256]{3,1,2,0:T(8,128)(2,1)S(1)}, u32[]{:S(2)}, u32[]{:S(2)}) async-start(bf16[16,8,16,256]{3,1,2,0:T(8,128)(2,1)} %copy.75), calls=%async_computation.1 | async-start | bytes 2097152 | tf_op jit(solution)/shard_map/all_to_all | solution.py:68
  45.2 29.9 %all-to-all-start = ((bf16[16,8,16,256]{3,1,2,0:T(8,128)(2,1)}), bf16[16,8,16,256]{3,1,2,0:T(8,128)(2,1)}, u32[]{:S(2)}, u32[]{:S(2)}) async-start(bf16[16,8,16,256]{3,1,2,0:T(8,128)(2,1)} %copy.73), calls=%async_computation | async-start | bytes 2097152 | tf_op jit(solution)/shard_map/all_to_all | solution.py:67
  52.3 24.7 %copy-start.2 = (bf16[1,8,16,16,256]{4,3,2,1,0:T(8,128)(2,1)}, bf16[1,8,16,16,256]{4,3,2,1,0:T(8,128)(2,1)S(1)}, u32[]{:S(2)}) copy-start(bf16[1,8,16,16,256]{4,3,2,1,0:T(8,128)(2,1)S(1)} %copy.76) | copy-start | bytes 3145732
  76.5 1.1 copy-start.1
  110.4 1.2 copy-start.7
  114.1 1.6 copy-start.5
  117.5 31.0 %copy-start.3 = (bf16[1,8,16,16,256]{4,3,2,1,0:T(8,128)(2,1)S(1)}, bf16[1,8,16,16,256]{4,3,2,1,0:T(8,128)(2,1)}, u32[]{:S(2)}) copy-start(bf16[1,8,16,16,256]{4,3,2,1,0:T(8,128)(2,1)} %copy-done.2) | copy-start | bytes 3145732
  147.3 1.0 copy-start.4
  150.6 28.0 %all-to-all-start.4 = ((bf16[1,8,256,256]{3,1,0,2:T(8,128)(2,1)}), bf16[1,8,256,256]{3,1,0,2:T(8,128)(2,1)}, u32[]{:S(2)}, u32[]{:S(2)}) async-start(bf16[1,8,256,256]{3,1,0,2:T(8,128)(2,1)} %copy.84), calls=%async_computation.4 | async-start | bytes 2097152 | tf_op jit(solution)/shard_map/all_to_all | solution.py:98
  178.6 29.9 %all-to-all-start.5 = ((bf16[1,8,256,256]{3,1,0,2:T(8,128)(2,1)}), bf16[1,8,256,256]{3,1,0,2:T(8,128)(2,1)}, u32[]{:S(2)}, u32[]{:S(2)}) async-start(bf16[1,8,256,256]{3,1,0,2:T(8,128)(2,1)} %copy.87), calls=%async_computation.5 | async-start | bytes 2097152 | tf_op jit(solution)/shard_map/all_to_all | solution.py:99
  185.5 124.0 %all-reduce.2.cloned.1.call-start = ((), (), s32[]{:S(2)}) async-start(), calls=%async_computation.6 | async-start | bytes 393216 | tf_op jit(solution)/shard_map/psum | solution.py:121
  185.8 2.0 copy-start.6
  214.8 1.2 copy-start.8
Sparse Core Ops, SparseCore 0:
  217.6 91.8 all-reduce.1
where the time goes:
time: 319 us; the launch traced here: 318 us
  waiting for transfers between devices  170 us (53%)
  blocking collectives  61.3 us (19%)
  starting transfers between devices  26.5 us (8%)
  local copies, waits for them, and re-layouts  16.9 us (5%)
  matrix products  16.5 us (5%)
  between operations  14.4 us (5%)
  other arithmetic  12.6 us (4%)
    psum x1, waiting for transfers between devices, body(): lax.psum(jnp.concatenate([in_weights, out_weights], axis=0).astype(jnp.bf...  88.2 us
    all_to_all x1, blocking collectives, body(): lax.all_to_all(products, 'rows', split_axis=2, concat_axis=0, tiled=True)  31.5 us
    all_to_all x1, blocking collectives, body(): lax.all_to_all(prod_grad, 'rows', split_axis=0, concat_axis=2, tiled=True)  29.8 us
    all_to_all x1, waiting for transfers between devices, body(): lax.all_to_all(left_edge, 'rows', split_axis=0, concat_axis=2, tiled=True)  22.8 us
    all_to_all x1, waiting for transfers between devices, body(): lax.all_to_all(right_edge, 'rows', split_axis=0, concat_axis=2, tiled=True)  21.9 us
    all_to_all x1, waiting for transfers between devices, body(): lax.all_to_all(left_part, 'rows', split_axis=2, concat_axis=0, tiled=True)  19.3 us
    all_to_all x1, waiting for transfers between devices, body(): lax.all_to_all(right_part, 'rows', split_axis=2, concat_axis=0, tiled=True)  17.8 us
    unnamed x23, local copies, waits for them, and re-layouts  8.91 us
  transfers between devices with their start and end apart: 5, of which 5 were waited for; matrix products, arithmetic and copies ran while one was open for 4% of the time, Pallas kernels for 0%

commit v1 on v0

--- a/solution.py
+++ b/solution.py
@@ -37,6 +37,26 @@
 
 
 def body(pair, proj_weights, cotangent):
+
+    def group_plane(array_in):
+        f_next, parts_out = (lax.axis_size("rows"), lax.axis_index("rows"))
+        state_next = list(array_in.shape)
+        n_now = array_in.shape[2] // f_next
+        state_next[2] = n_now
+        b_next = state_next[0]
+        state_next[0] = b_next * f_next
+        u_next = jnp.zeros(state_next, array_in.dtype)
+        for dev_i in range(f_next):
+            y1 = lax.dynamic_slice_in_dim(array_in, (parts_out ^ dev_i) * n_now, n_now, axis=2)
+            if dev_i:
+                y1 = lax.ppermute(
+                    y1, axis_name="rows", perm=list(map(lambda no: (no, no ^ dev_i), range(f_next)))
+                )
+            u_next = lax.dynamic_update_slice_in_dim(
+                u_next, y1, (parts_out ^ dev_i) * b_next, axis=0
+            )
+        return u_next
+
     residues = pair.shape[1]
     local_rows = pair.shape[0]
     chans = pair.shape[2]
@@ -96,7 +116,7 @@
     left_part, right_part = edge_backward(slab_grad, left_held, right_held)
     left_back, right_back = (
         lax.all_to_all(left_part, "rows", split_axis=2, concat_axis=0, tiled=True),
-        lax.all_to_all(right_part, "rows", split_axis=2, concat_axis=0, tiled=True),
+        group_plane(right_part),
     )
     left_full = left_back.reshape(chans, local_rows, residues).astype(jnp.float32)
     right_full = right_back.reshape(chans, local_rows, residues).astype(jnp.float32)

time: 319 us -> 334 us (1.047)
  waiting for transfers between devices: 170 us -> 201 us
  blocking collectives: 61.3 us -> 31.5 us
  starting transfers between devices: 26.5 us -> 40 us
    ppermute x0 -> x15, waiting for transfers between devices: none -> 53.6 us  [group_plane(): lax.ppermute(y1, axis_name='rows', perm=list(map(lambda no: (no, no ^ dev...]
    all_to_all x1 -> x0, blocking collectives: 29.8 us -> none  [body(): lax.all_to_all(prod_grad, 'rows', split_axis=0, concat_axis=2, tiled=True)]
    all_to_all x1, waiting for transfers between devices: 19.3 us -> 0.01 us  [body(): lax.all_to_all(left_part, 'rows', split_axis=2, concat_axis=0, tiled=True)]
    ppermute x0 -> x15, starting transfers between devices: none -> 13.8 us  [group_plane(): lax.ppermute(y1, axis_name='rows', perm=list(map(lambda no: (no, no ^ dev...]
    unnamed x23 -> x21, local copies, waits for them, and re-layouts: 8.91 us -> 7.89 us
  transfers between devices with their start and end apart: 5 -> 20, of which waited for: 5 -> 15; matrix products, arithmetic and copies ran while one was open for 4% -> 3% of each run, Pallas kernels for 0% -> 0%
where the time goes in v1:
time: 334 us; the launch traced here: 333 us
  waiting for transfers between devices  201 us (60%)
  starting transfers between devices  40 us (12%)
  blocking collectives  31.5 us (9%)
  local copies, waits for them, and re-layouts  17.2 us (5%)
  matrix products  16.6 us (5%)
  between operations  14.8 us (4%)
  other arithmetic  12.1 us (4%)
    psum x1, waiting for transfers between devices, body(): lax.psum(jnp.concatenate([in_weights, out_weights], axis=0).astype(jnp.bf...  85.1 us
    ppermute x15, waiting for transfers between devices, group_plane(): lax.ppermute(y1, axis_name='rows', perm=list(map(lambda no: (no, no ^ dev...  53.6 us
    all_to_all x1, blocking collectives, body(): lax.all_to_all(products, 'rows', split_axis=2, concat_axis=0, tiled=True)  31.5 us
    all_to_all x1, waiting for transfers between devices, body(): lax.all_to_all(left_edge, 'rows', split_axis=0, concat_axis=2, tiled=True)  22.8 us
    all_to_all x1, waiting for transfers between devices, body(): lax.all_to_all(right_edge, 'rows', split_axis=0, concat_axis=2, tiled=True)  21.9 us
    all_to_all x1, waiting for transfers between devices, body(): lax.all_to_all(prod_grad, 'rows', split_axis=0, concat_axis=2, tiled=True)  17.9 us
    ppermute x15, starting transfers between devices, group_plane(): lax.ppermute(y1, axis_name='rows', perm=list(map(lambda no: (no, no ^ dev...  13.8 us
    unnamed x21, local copies, waits for them, and re-layouts  7.89 us
  transfers between devices with their start and end apart: 20, of which 15 were waited for; matrix products, arithmetic and copies ran while one was open for 3% of the time, Pallas kernels for 0%

profile of v1, /device:TPU:0, one launch (start us, length us, event | category | flops | bytes accessed | tf_op | source)
XLA Modules:
  0.0 333.5 jit_solution(10166912345963689288)
XLA Ops:
  11.7 2.0 copy-done
  14.8 7.4 %all-to-all-start.1 = ((bf16[16,8,16,256]{3,1,2,0:T(8,128)(2,1)}), bf16[16,8,16,256]{3,1,2,0:T(8,128)(2,1)S(1)}, u32[]{:S(2)}, u32[]{:S(2)}) async-start(bf16[16,8,16,256]{3,1,2,0:T(8,128)(2,1)} %copy.103), calls=%async_computation.1 | async-start | bytes 2097152 | tf_op jit(solution)/shard_map/all_to_all | solution.py:88
  23.3 21.9 %all-to-all-done.1 = bf16[16,8,16,256]{3,1,2,0:T(8,128)(2,1)S(1)} async-done(((bf16[16,8,16,256]{3,1,2,0:T(8,128)(2,1)}), bf16[16,8,16,256]{3,1,2,0:T(8,128)(2,1)S(1)}, u32[]{:S(2)}, u32[]{:S(2)}) %all-to-all-start.1) | async-done | bytes 1048608 | tf_op jit(solution)/shard_map/all_to_all | solution.py:88
  45.2 6.9 %all-to-all-start = ((bf16[16,8,16,256]{3,1,2,0:T(8,128)(2,1)}), bf16[16,8,16,256]{3,1,2,0:T(8,128)(2,1)}, u32[]{:S(2)}, u32[]{:S(2)}) async-start(bf16[16,8,16,256]{3,1,2,0:T(8,128)(2,1)} %copy.101), calls=%async_computation | async-start | bytes 2097152 | tf_op jit(solution)/shard_map/all_to_all | solution.py:87
  52.3 22.8 %all-to-all-done = bf16[16,8,16,256]{3,1,2,0:T(8,128)(2,1)} async-done(((bf16[16,8,16,256]{3,1,2,0:T(8,128)(2,1)}), bf16[16,8,16,256]{3,1,2,0:T(8,128)(2,1)}, u32[]{:S(2)}, u32[]{:S(2)}) %all-to-all-start) | async-done | bytes 1048608 | tf_op jit(solution)/shard_map/all_to_all | solution.py:87
  77.6 31.5 %all_to_all.63 = bf16[1,8,256,256]{3,1,0,2:T(8,128)(2,1)S(1)} all-to-all(bf16[1,8,256,256]{3,1,0,2:T(8,128)(2,1)S(1)} %copy.105), channel_id=1, replica_groups=mesh['groups'=2,'rows'=16] {'rows'}, dimensions={2} | all-to-all | bytes 2097152 | tf_op jit(solution)/shard_map/all_to_all | solution.py:91
  111.6 2.5 fusion.13
  114.2 1.6 bitcast_reduce_fusion
  115.8 1.6 fusion.46
  118.5 5.0 %all-to-all-start.3 = ((bf16[16,8,16,256]{3,1,2,0:T(8,128)(2,1)}), bf16[16,8,16,256]{3,1,2,0:T(8,128)(2,1)}, u32[]{:S(2)}, u32[]{:S(2)}) async-start(bf16[16,8,16,256]{3,1,2,0:T(8,128)(2,1)} %copy.110), calls=%async_computation.3 | async-start | bytes 2097152 | tf_op jit(solution)/shard_map/all_to_all | solution.py:115
  123.8 2.0 fusion.42
  125.8 2.9 fusion.41
  128.7 17.9 %all-to-all-done.3 = bf16[16,8,16,256]{3,1,2,0:T(8,128)(2,1)} async-done(((bf16[16,8,16,256]{3,1,2,0:T(8,128)(2,1)}), bf16[16,8,16,256]{3,1,2,0:T(8,128)(2,1)}, u32[]{:S(2)}, u32[]{:S(2)}) %all-to-all-start.3) | async-done | bytes 1048608 | tf_op jit(solution)/shard_map/all_to_all | solution.py:115
  146.6 2.1 convolution_convert_fusion
  150.6 1.6 copy.112
  152.2 6.9 %all-to-all-start.4 = ((bf16[1,8,256,256]{3,1,0,2:T(8,128)(2,1)}), bf16[1,8,256,256]{3,1,0,2:T(8,128)(2,1)S(1)}, u32[]{:S(2)}, u32[]{:S(2)}) async-start(bf16[1,8,256,256]{3,1,0,2:T(8,128)(2,1)} %copy.112), calls=%async_computation.4 | async-start | bytes 2097152 | tf_op jit(solution)/shard_map/all_to_all | solution.py:118
  159.3 4.4 %collective-permute-start.14 = (bf16[1,8,16,256]{3,2,1,0:T(8,128)(2,1)S(1)}, bf16[1,8,16,256]{3,2,1,0:T(8,128)(2,1)S(1)}, u32[]{:S(2)}, u32[]{:S(2)}) collective-permute-start(bf16[1,8,16,256]{3,2,1,0:T(8,128)(2,1)S(1)} %get-tuple-element.29), channel_id=1, source_target_pairs={{0,15},{1,14},{2,13},{3,12},{4,11},{5,10},{6,9},{7,8},{8,7},{9,6},... | collective-permute-start | bytes 196616 | tf_op jit(solution)/shard_map/ppermute | solution.py:52
  164.2 3.1 collective-permute-start.12
  168.9 1.7 collective-permute-start.1
  170.6 4.1 %collective-permute-done.1 = bf16[1,8,16,256]{3,2,1,0:T(8,128)(2,1)S(1)} collective-permute-done((bf16[1,8,16,256]{3,2,1,0:T(8,128)(2,1)S(1)}, bf16[1,8,16,256]{3,2,1,0:T(8,128)(2,1)S(1)}, u32[]{:S(2)}, u32[]{:S(2)}) %collective-permute-start.1) | collective-permute-done | bytes 65568 | tf_op jit(solution)/shard_map/ppermute | solution.py:52
  174.7 4.3 %collective-permute-done.2 = bf16[1,8,16,256]{3,2,1,0:T(8,128)(2,1)S(1)} collective-permute-done((bf16[1,8,16,256]{3,2,1,0:T(8,128)(2,1)S(1)}, bf16[1,8,16,256]{3,2,1,0:T(8,128)(2,1)S(1)}, u32[]{:S(2)}, u32[]{:S(2)}) %collective-permute-start.2) | collective-permute-done | bytes 65568 | tf_op jit(solution)/shard_map/ppermute | solution.py:52
  179.0 10.9 %collective-permute-done.3 = bf16[1,8,16,256]{3,2,1,0:T(8,128)(2,1)S(1)} collective-permute-done((bf16[1,8,16,256]{3,2,1,0:T(8,128)(2,1)S(1)}, bf16[1,8,16,256]{3,2,1,0:T(8,128)(2,1)S(1)}, u32[]{:S(2)}, u32[]{:S(2)}) %collective-permute-start.3) | collective-permute-done | bytes 65568 | tf_op jit(solution)/shard_map/ppermute | solution.py:52
  189.9 4.1 %collective-permute-done.4 = bf16[1,8,16,256]{3,2,1,0:T(8,128)(2,1)S(1)} collective-permute-done((bf16[1,8,16,256]{3,2,1,0:T(8,128)(2,1)S(1)}, bf16[1,8,16,256]{3,2,1,0:T(8,128)(2,1)S(1)}, u32[]{:S(2)}, u32[]{:S(2)}) %collective-permute-start.4) | collective-permute-done | bytes 65568 | tf_op jit(solution)/shard_map/ppermute | solution.py:52
  194.8 4.5 %collective-permute-done.5 = bf16[1,8,16,256]{3,2,1,0:T(8,128)(2,1)S(1)} collective-permute-done((bf16[1,8,16,256]{3,2,1,0:T(8,128)(2,1)S(1)}, bf16[1,8,16,256]{3,2,1,0:T(8,128)(2,1)S(1)}, u32[]{:S(2)}, u32[]{:S(2)}) %collective-permute-start.5) | collective-permute-done | bytes 65568 | tf_op jit(solution)/shard_map/ppermute | solution.py:52
  199.4 4.4 %collective-permute-done.6 = bf16[1,8,16,256]{3,2,1,0:T(8,128)(2,1)S(1)} collective-permute-done((bf16[1,8,16,256]{3,2,1,0:T(8,128)(2,1)S(1)}, bf16[1,8,16,256]{3,2,1,0:T(8,128)(2,1)S(1)}, u32[]{:S(2)}, u32[]{:S(2)}) %collective-permute-start.6) | collective-permute-done | bytes 65568 | tf_op jit(solution)/shard_map/ppermute | solution.py:52
  205.1 4.5 %collective-permute-done.7 = bf16[1,8,16,256]{3,2,1,0:T(8,128)(2,1)S(1)} collective-permute-done((bf16[1,8,16,256]{3,2,1,0:T(8,128)(2,1)S(1)}, bf16[1,8,16,256]{3,2,1,0:T(8,128)(2,1)S(1)}, u32[]{:S(2)}, u32[]{:S(2)}) %collective-permute-start.7) | collective-permute-done | bytes 65568 | tf_op jit(solution)/shard_map/ppermute | solution.py:52
  209.6 5.3 %collective-permute-done.8 = bf16[1,8,16,256]{3,2,1,0:T(8,128)(2,1)S(1)} collective-permute-done((bf16[1,8,16,256]{3,2,1,0:T(8,128)(2,1)S(1)}, bf16[1,8,16,256]{3,2,1,0:T(8,128)(2,1)S(1)}, u32[]{:S(2)}, u32[]{:S(2)}) %collective-permute-start.8) | collective-permute-done | bytes 65568 | tf_op jit(solution)/shard_map/ppermute | solution.py:52
  216.5 4.5 %collective-permute-done.9 = bf16[1,8,16,256]{3,2,1,0:T(8,128)(2,1)S(1)} collective-permute-done((bf16[1,8,16,256]{3,2,1,0:T(8,128)(2,1)S(1)}, bf16[1,8,16,256]{3,2,1,0:T(8,128)(2,1)S(1)}, u32[]{:S(2)}, u32[]{:S(2)}) %collective-permute-start.9) | collective-permute-done | bytes 65568 | tf_op jit(solution)/shard_map/ppermute | solution.py:52
  221.1 6.1 %collective-permute-done.10 = bf16[1,8,16,256]{3,2,1,0:T(8,128)(2,1)S(1)} collective-permute-done((bf16[1,8,16,256]{3,2,1,0:T(8,128)(2,1)S(1)}, bf16[1,8,16,256]{3,2,1,0:T(8,128)(2,1)S(1)}, u32[]{:S(2)}, u32[]{:S(2)}) %collective-permute-start.10) | collective-permute-done | bytes 65568 | tf_op jit(solution)/shard_map/ppermute | solution.py:52
  227.4 4.4 %fusion.24 = (bf16[1,128,16,256]{3,1,0,2:T(8,128)(2,1)S(1)}, bf16[1,128,16,256]{3,1,0,2:T(8,128)(2,1)S(1)}, bf16[1,128,16,256]{3,1,0,2:T(8,128)(2,1)S(1)}, bf16[1,128,16,256]{3,1,0,2:T(8,128)(2,1)S(1)}) fusion(f32[4,128,16,256]{3,1,0,2:T(8,128)} %copy-done, bf16[16,8,16,256]{3,1,0,2:T(8,128)(2,1)S(1)} %copy_dynamic-update-slice_fusion, ...), kind=kLoop, calls=%fused_computation.37 | loop fusion | flops 11534336 | bytes 14680064 | tf_op jit(solution)/shard_map/convert.15
  237.3 2.3 copy.135
  239.6 85.1 %all-reduce.2.cloned.1.call-done = bf16[6,128,128]{1,2,0:T(8,128)(2,1)} async-done(((bf16[6,128,128]{1,2,0:T(8,128)(2,1)}), bf16[6,128,128]{1,2,0:T(8,128)(2,1)}) %all-reduce.2.cloned.1.call-update) | async-done | bytes 196624 | tf_op jit(solution)/shard_map/psum | solution.py:141
  (89 shorter events, 28.3 us)
Async XLA Ops:
  7.2 2.1 copy-start.8
  10.5 3.2 copy-start
  14.8 30.3 %all-to-all-start.1 = ((bf16[16,8,16,256]{3,1,2,0:T(8,128)(2,1)}), bf16[16,8,16,256]{3,1,2,0:T(8,128)(2,1)S(1)}, u32[]{:S(2)}, u32[]{:S(2)}) async-start(bf16[16,8,16,256]{3,1,2,0:T(8,128)(2,1)} %copy.103), calls=%async_computation.1 | async-start | bytes 2097152 | tf_op jit(solution)/shard_map/all_to_all | solution.py:88
  45.2 29.9 %all-to-all-start = ((bf16[16,8,16,256]{3,1,2,0:T(8,128)(2,1)}), bf16[16,8,16,256]{3,1,2,0:T(8,128)(2,1)}, u32[]{:S(2)}, u32[]{:S(2)}) async-start(bf16[16,8,16,256]{3,1,2,0:T(8,128)(2,1)} %copy.101), calls=%async_computation | async-start | bytes 2097152 | tf_op jit(solution)/shard_map/all_to_all | solution.py:87
  52.3 24.7 %copy-start.1 = (bf16[1,8,16,16,256]{4,3,2,1,0:T(8,128)(2,1)}, bf16[1,8,16,16,256]{4,3,2,1,0:T(8,128)(2,1)S(1)}, u32[]{:S(2)}) copy-start(bf16[1,8,16,16,256]{4,3,2,1,0:T(8,128)(2,1)S(1)} %copy.104) | copy-start | bytes 3145732
  76.5 1.1 copy-start.3
  110.4 1.2 copy-start.6
  114.2 1.6 copy-start.4
  118.5 28.0 %all-to-all-start.3 = ((bf16[16,8,16,256]{3,1,2,0:T(8,128)(2,1)}), bf16[16,8,16,256]{3,1,2,0:T(8,128)(2,1)}, u32[]{:S(2)}, u32[]{:S(2)}) async-start(bf16[16,8,16,256]{3,1,2,0:T(8,128)(2,1)} %copy.110), calls=%async_computation.3 | async-start | bytes 2097152 | tf_op jit(solution)/shard_map/all_to_all | solution.py:115
  123.8 2.0 copy-start.5
  146.6 3.6 %copy-start.2 = (bf16[1,8,16,16,256]{4,3,2,1,0:T(8,128)(2,1)S(1)}, bf16[1,8,16,16,256]{4,3,2,1,0:T(8,128)(2,1)}, u32[]{:S(2)}) copy-start(bf16[1,8,16,16,256]{4,3,2,1,0:T(8,128)(2,1)} %copy-done.1) | copy-start | bytes 3145732
  152.2 75.1 %all-to-all-start.4 = ((bf16[1,8,256,256]{3,1,0,2:T(8,128)(2,1)}), bf16[1,8,256,256]{3,1,0,2:T(8,128)(2,1)S(1)}, u32[]{:S(2)}, u32[]{:S(2)}) async-start(bf16[1,8,256,256]{3,1,0,2:T(8,128)(2,1)} %copy.112), calls=%async_computation.4 | async-start | bytes 2097152 | tf_op jit(solution)/shard_map/all_to_all | solution.py:118
  159.1 165.6 %all-reduce.2.cloned.1.call-start = ((), (), s32[]{:S(2)}) async-start(), calls=%async_computation.5 | async-start | bytes 393216 | tf_op jit(solution)/shard_map/psum | solution.py:141
  159.3 68.0 %collective-permute-start.14 = (bf16[1,8,16,256]{3,2,1,0:T(8,128)(2,1)S(1)}, bf16[1,8,16,256]{3,2,1,0:T(8,128)(2,1)S(1)}, u32[]{:S(2)}, u32[]{:S(2)}) collective-permute-start(bf16[1,8,16,256]{3,2,1,0:T(8,128)(2,1)S(1)} %get-tuple-element.29), channel_id=1, source_target_pairs={{0,15},{1,14},{2,13},{3,12},{4,11},{5,10},{6,9},{7,8},{8,7},{9,6},... | collective-permute-start | bytes 196616 | tf_op jit(solution)/shard_map/ppermute | solution.py:52
  163.8 63.5 %collective-permute-start.13 = (bf16[1,8,16,256]{3,2,1,0:T(8,128)(2,1)S(1)}, bf16[1,8,16,256]{3,2,1,0:T(8,128)(2,1)S(1)}, u32[]{:S(2)}, u32[]{:S(2)}) collective-permute-start(bf16[1,8,16,256]{3,2,1,0:T(8,128)(2,1)S(1)} %get-tuple-element.30), channel_id=1, source_target_pairs={{0,14},{1,15},{2,12},{3,13},{4,10},{5,11},{6,8},{7,9},{8,6},{9,7},... | collective-permute-start | bytes 196616 | tf_op jit(solution)/shard_map/ppermute | solution.py:52
  164.2 63.1 %collective-permute-start.12 = (bf16[1,8,16,256]{3,2,1,0:T(8,128)(2,1)S(1)}, bf16[1,8,16,256]{3,2,1,0:T(8,128)(2,1)S(1)}, u32[]{:S(2)}, u32[]{:S(2)}) collective-permute-start(bf16[1,8,16,256]{3,2,1,0:T(8,128)(2,1)S(1)} %get-tuple-element.31), channel_id=1, source_target_pairs={{0,13},{1,12},{2,15},{3,14},{4,9},{5,8},{6,11},{7,10},{8,5},{9,4},... | collective-permute-start | bytes 196616 | tf_op jit(solution)/shard_map/ppermute | solution.py:52
  167.3 59.9 %collective-permute-start.11 = (bf16[1,8,16,256]{3,2,1,0:T(8,128)(2,1)S(1)}, bf16[1,8,16,256]{3,2,1,0:T(8,128)(2,1)S(1)}, u32[]{:S(2)}, u32[]{:S(2)}) collective-permute-start(bf16[1,8,16,256]{3,2,1,0:T(8,128)(2,1)S(1)} %get-tuple-element.32), channel_id=1, source_target_pairs={{0,12},{1,13},{2,14},{3,15},{4,8},{5,9},{6,10},{7,11},{8,4},{9,5},... | collective-permute-start | bytes 196616 | tf_op jit(solution)/shard_map/ppermute | solution.py:52
  167.6 1.3 collective-permute-start
  168.9 5.8 %collective-permute-start.1 = (bf16[1,8,16,256]{3,2,1,0:T(8,128)(2,1)S(1)}, bf16[1,8,16,256]{3,2,1,0:T(8,128)(2,1)S(1)}, u32[]{:S(2)}, u32[]{:S(2)}) collective-permute-start(bf16[1,8,16,256]{3,2,1,0:T(8,128)(2,1)S(1)} %get-tuple-element.42), channel_id=1, source_target_pairs={{0,2},{1,3},{2,0},{3,1},{4,6},{5,7},{6,4},{7,5},{8,10},{9,11},{10,... | collective-permute-start | bytes 196616 | tf_op jit(solution)/shard_map/ppermute | solution.py:52
  174.7 4.3 %collective-permute-start.2 = (bf16[1,8,16,256]{3,2,1,0:T(8,128)(2,1)S(1)}, bf16[1,8,16,256]{3,2,1,0:T(8,128)(2,1)S(1)}, u32[]{:S(2)}, u32[]{:S(2)}) collective-permute-start(bf16[1,8,16,256]{3,2,1,0:T(8,128)(2,1)S(1)} %get-tuple-element.41), channel_id=1, source_target_pairs={{0,3},{1,2},{2,1},{3,0},{4,7},{5,6},{6,5},{7,4},{8,11},{9,10},{10,... | collective-permute-start | bytes 196616 | tf_op jit(solution)/shard_map/ppermute | solution.py:52
  179.0 10.9 %collective-permute-start.3 = (bf16[1,8,16,256]{3,2,1,0:T(8,128)(2,1)S(1)}, bf16[1,8,16,256]{3,2,1,0:T(8,128)(2,1)S(1)}, u32[]{:S(2)}, u32[]{:S(2)}) collective-permute-start(bf16[1,8,16,256]{3,2,1,0:T(8,128)(2,1)S(1)} %get-tuple-element.40), channel_id=1, source_target_pairs={{0,4},{1,5},{2,6},{3,7},{4,0},{5,1},{6,2},{7,3},{8,12},{9,13},{10,... | collective-permute-start | bytes 196616 | tf_op jit(solution)/shard_map/ppermute | solution.py:52
  189.9 4.2 %collective-permute-start.4 = (bf16[1,8,16,256]{3,2,1,0:T(8,128)(2,1)S(1)}, bf16[1,8,16,256]{3,2,1,0:T(8,128)(2,1)S(1)}, u32[]{:S(2)}, u32[]{:S(2)}) collective-permute-start(bf16[1,8,16,256]{3,2,1,0:T(8,128)(2,1)S(1)} %get-tuple-element.39), channel_id=1, source_target_pairs={{0,5},{1,4},{2,7},{3,6},{4,1},{5,0},{6,3},{7,2},{8,13},{9,12},{10,... | collective-permute-start | bytes 196616 | tf_op jit(solution)/shard_map/ppermute | solution.py:52
  194.1 5.2 %collective-permute-start.5 = (bf16[1,8,16,256]{3,2,1,0:T(8,128)(2,1)S(1)}, bf16[1,8,16,256]{3,2,1,0:T(8,128)(2,1)S(1)}, u32[]{:S(2)}, u32[]{:S(2)}) collective-permute-start(bf16[1,8,16,256]{3,2,1,0:T(8,128)(2,1)S(1)} %get-tuple-element.38), channel_id=1, source_target_pairs={{0,6},{1,7},{2,4},{3,5},{4,2},{5,3},{6,0},{7,1},{8,14},{9,15},{10,... | collective-permute-start | bytes 196616 | tf_op jit(solution)/shard_map/ppermute | solution.py:52
  199.2 4.6 %collective-permute-start.6 = (bf16[1,8,16,256]{3,2,1,0:T(8,128)(2,1)S(1)}, bf16[1,8,16,256]{3,2,1,0:T(8,128)(2,1)S(1)}, u32[]{:S(2)}, u32[]{:S(2)}) collective-permute-start(bf16[1,8,16,256]{3,2,1,0:T(8,128)(2,1)S(1)} %get-tuple-element.37), channel_id=1, source_target_pairs={{0,7},{1,6},{2,5},{3,4},{4,3},{5,2},{6,1},{7,0},{8,15},{9,14},{10,... | collective-permute-start | bytes 196616 | tf_op jit(solution)/shard_map/ppermute | solution.py:52
  203.8 5.8 %collective-permute-start.7 = (bf16[1,8,16,256]{3,2,1,0:T(8,128)(2,1)S(1)}, bf16[1,8,16,256]{3,2,1,0:T(8,128)(2,1)S(1)}, u32[]{:S(2)}, u32[]{:S(2)}) collective-permute-start(bf16[1,8,16,256]{3,2,1,0:T(8,128)(2,1)S(1)} %get-tuple-element.36), channel_id=1, source_target_pairs={{0,8},{1,9},{2,10},{3,11},{4,12},{5,13},{6,14},{7,15},{8,0},{9,1},... | collective-permute-start | bytes 196616 | tf_op jit(solution)/shard_map/ppermute | solution.py:52
  209.6 5.4 %collective-permute-start.8 = (bf16[1,8,16,256]{3,2,1,0:T(8,128)(2,1)S(1)}, bf16[1,8,16,256]{3,2,1,0:T(8,128)(2,1)S(1)}, u32[]{:S(2)}, u32[]{:S(2)}) collective-permute-start(bf16[1,8,16,256]{3,2,1,0:T(8,128)(2,1)S(1)} %get-tuple-element.35), channel_id=1, source_target_pairs={{0,9},{1,8},{2,11},{3,10},{4,13},{5,12},{6,15},{7,14},{8,1},{9,0},... | collective-permute-start | bytes 196616 | tf_op jit(solution)/shard_map/ppermute | solution.py:52
  215.0 6.1 %collective-permute-start.9 = (bf16[1,8,16,256]{3,2,1,0:T(8,128)(2,1)S(1)}, bf16[1,8,16,256]{3,2,1,0:T(8,128)(2,1)S(1)}, u32[]{:S(2)}, u32[]{:S(2)}) collective-permute-start(bf16[1,8,16,256]{3,2,1,0:T(8,128)(2,1)S(1)} %get-tuple-element.34), channel_id=1, source_target_pairs={{0,10},{1,11},{2,8},{3,9},{4,14},{5,15},{6,12},{7,13},{8,2},{9,3},... | collective-permute-start | bytes 196616 | tf_op jit(solution)/shard_map/ppermute | solution.py:52
  221.0 6.1 %collective-permute-start.10 = (bf16[1,8,16,256]{3,2,1,0:T(8,128)(2,1)S(1)}, bf16[1,8,16,256]{3,2,1,0:T(8,128)(2,1)S(1)}, u32[]{:S(2)}, u32[]{:S(2)}) collective-permute-start(bf16[1,8,16,256]{3,2,1,0:T(8,128)(2,1)S(1)} %get-tuple-element.33), channel_id=1, source_target_pairs={{0,11},{1,10},{2,9},{3,8},{4,15},{5,14},{6,13},{7,12},{8,3},{9,2},... | collective-permute-start | bytes 196616 | tf_op jit(solution)/shard_map/ppermute | solution.py:52
  233.1 1.2 copy-start.7
Sparse Core Ops, SparseCore 0:
  235.9 88.8 all-reduce.1
